TPU v7x, 32 devices: a whole 2x2x4 slice. The times are simulated.
32 devices in a mesh: row: 4 (over y, x), col: 8 (over z, core).
Axes of the slice: x: 2, y: 2, z: 4, core: 2. Of those that a mesh axis runs over, the one named last changes fastest.
Arguments:
- upper_tiles: bfloat16 [256, 5, 256, 256], P('row', None, 'col'), may hold values from -0.8984375 to 0.8984375
- occupied: int32 [256, 4], P(('row', 'col')), may hold values from 0 to 1, as said below
Outputs:
- square_tiles: bfloat16 [256, 5, 256, 256], P('row', None, 'col')
Inputs may be any that keep to these rules, and one draw needn't show every extreme that they name: Occupancy; its density differs between aligned groups of 8 block rows, and the diagonal block is always occupied (not listed).
All inputs are finite; a program needn't handle non-finite values.
Results may differ from a plain program's by a relative error of at most 0.0024.
Values may be sent and summed in bfloat16 or wider, within the bound.
A program may use at most 256 MiB of HBM per device.

v0:
```python
import jax
import jax.numpy as jnp
from jax import lax
from jax.sharding import PartitionSpec as P


def extended_2(cells, sides, width):
    for axis, dim in sides:
        count = lax.axis_size(axis)
        ends = count - 1
        head = lax.slice_in_dim(cells, 0, width, axis=dim)
        tail = lax.slice_in_dim(cells, cells.shape[dim] - width, cells.shape[dim], axis=dim)
        cells = jnp.concatenate(
            [
                lax.ppermute(tail, axis, [(i, (i + 1) % count) for i in range(ends)]),
                cells,
                lax.ppermute(head, axis, [((i + 1) % count, i) for i in range(ends)]),
            ],
            axis=dim,
        )
    return cells


def build_band(tiles_here, occupied, first_row, total_rows):
    block_rows = occupied.shape[0]
    band_width = occupied.shape[1]
    row_index = first_row + jnp.arange(block_rows, dtype=jnp.int32)
    offsets = jnp.arange(1, band_width + 1, dtype=jnp.int32)
    kept_mask = (occupied == 1) & (row_index[:, None] + offsets[None, :] < total_rows)
    diag_full = tiles_here[:, 0].astype(jnp.float32)
    diag_tile = (0.5 * (diag_full + jnp.swapaxes(diag_full, 1, 2))).astype(jnp.bfloat16)
    off_tiles = jnp.where(
        kept_mask[:, :, None, None], tiles_here[:, 1:], jnp.zeros((), jnp.bfloat16)
    )
    return (jnp.concatenate([diag_tile[:, None], off_tiles], axis=1), kept_mask)


def square_band(extended, kept_mask, block_rows, band_width):
    results = []
    for column_shift in range(band_width + 1):
        lefts = []
        rights = []
        for inner in range(column_shift - band_width, band_width + 1):
            start = band_width + inner
            if inner >= 0:
                left = extended[band_width : band_width + block_rows, inner]
            else:
                left = jnp.swapaxes(extended[start : start + block_rows, -inner], 1, 2)
            rest = column_shift - inner
            if rest >= 0:
                right = extended[start : start + block_rows, rest]
            else:
                lower = band_width + column_shift
                right = jnp.swapaxes(extended[lower : lower + block_rows, -rest], 1, 2)
            lefts.append(left)
            rights.append(right)
        left_stack = jnp.stack(lefts, axis=1)
        right_stack = jnp.stack(rights, axis=1)
        summed = jnp.einsum(
            "rkab,rkbc->rac", left_stack, right_stack, preferred_element_type=jnp.float32
        )
        if column_shift > 0:
            summed = jnp.where(
                kept_mask[:, column_shift - 1, None, None], summed, jnp.zeros((), jnp.float32)
            )
        results.append(summed.astype(jnp.bfloat16))
    return jnp.stack(results, axis=1)


def shards(upper_tiles, occupied):
    tiles_here = lax.all_to_all(upper_tiles, "col", split_axis=0, concat_axis=2, tiled=True)
    block_rows = occupied.shape[0]
    band_width = occupied.shape[1]
    device_count = lax.axis_size("row") * lax.axis_size("col")
    position = lax.axis_index("row") * lax.axis_size("col") + lax.axis_index("col")
    band, kept_mask = build_band(
        tiles_here, occupied, position * block_rows, block_rows * device_count
    )
    extended = extended_2(band, ((("row", "col"), 0),), band_width)
    product = square_band(extended, kept_mask, block_rows, band_width)
    return lax.all_to_all(product, "col", split_axis=2, concat_axis=0, tiled=True)


def solution(mesh):
    return jax.shard_map(
        shards,
        mesh=mesh,
        in_specs=(P("row", None, "col", None), P(("row", "col"), None)),
        out_specs=P("row", None, "col", None),
        check_vma=False,
    )
```

profile of v0, /device:TPU:11, one launch (start us, length us, event | category | flops | bytes accessed | tf_op | source)
XLA Modules:
  0.0 487.5 jit_solution(7131705204764250208)
XLA Ops:
  0.0 5.8 %all-to-all-start = ((bf16[64,5,32,256]{3,2,1,0:T(8,128)(2,1)}), bf16[64,5,32,256]{3,2,1,0:T(8,128)(2,1)}, u32[]{:S(2)}, u32[]{:S(2)}) async-start(bf16[64,5,32,256]{3,2,1,0:T(8,128)(2,1)} %param.2), calls=%async_computation | async-start | bytes 10485760 | tf_op jit(solution)/shard_map/all_to_all | solution.py:71
  5.9 112.8 %all-to-all-done = bf16[64,5,32,256]{3,2,1,0:T(8,128)(2,1)} async-done(((bf16[64,5,32,256]{3,2,1,0:T(8,128)(2,1)}), bf16[64,5,32,256]{3,2,1,0:T(8,128)(2,1)}, u32[]{:S(2)}, u32[]{:S(2)}) %all-to-all-start) | async-done | bytes 5242912 | tf_op jit(solution)/shard_map/all_to_all | solution.py:71
  118.7 3.3 copy.102
  124.3 2.9 copy_select_fusion
  127.3 6.2 %copy.107 = bf16[8,4,256,256]{2,3,0,1:T(8,128)(2,1)} copy(bf16[8,4,256,256]{3,2,0,1:T(8,128)(2,1)} %copy_select_fusion) | data formatting | bytes 8388608 | tf_op jit(solution)/shard_map/jit(_where)/select_n | solution.py:32
  138.4 2.6 fusion.17
  141.0 2.4 collective-permute-start.1
  143.3 3.4 collective-permute-start
  147.8 46.1 %collective-permute-done.1 = bf16[4,5,256,256]{2,3,0,1:T(8,128)(2,1)S(1)} collective-permute-done((bf16[4,5,256,256]{2,3,0,1:T(8,128)(2,1)S(1)}, bf16[4,5,256,256]{2,3,0,1:T(8,128)(2,1)S(1)}, u32[]{:S(2)}, u32[]{:S(2)}) %collective-permute-start.1) | collective-permute-done | bytes 2621472 | tf_op jit(solution)/shard_map/ppermute | solution.py:17
  193.9 9.3 %collective-permute-done = bf16[4,5,256,256]{2,3,0,1:T(8,128)(2,1)S(1)} collective-permute-done((bf16[4,5,256,256]{2,3,0,1:T(8,128)(2,1)S(1)}, bf16[4,5,256,256]{2,3,0,1:T(8,128)(2,1)S(1)}, u32[]{:S(2)}, u32[]{:S(2)}) %collective-permute-start) | collective-permute-done | bytes 2621472 | tf_op jit(solution)/shard_map/ppermute | solution.py:15
  212.4 4.0 fusion.51
  216.4 2.3 copy.109
  218.7 2.3 constant_dynamic-update-slice_fusion.11
  220.9 2.3 copy.110
  223.2 2.3 copy.111
  225.6 2.3 copy.112
  227.8 3.1 constant_dynamic-update-slice_fusion.15
  230.9 3.1 constant_dynamic-update-slice_fusion.14
  234.0 2.3 constant_dynamic-update-slice_fusion.2
  238.5 2.3 constant_dynamic-update-slice_fusion.24
  240.8 2.3 copy.117
  243.1 2.3 constant_dynamic-update-slice_fusion.19
  245.3 2.3 copy.118
  248.9 2.3 constant_dynamic-update-slice_fusion.18
  251.2 2.3 constant_dynamic-update-slice_fusion.17
  253.5 4.4 slice_dynamic-update-slice_fusion.8
  257.9 2.3 copy.113
  260.2 2.3 copy.114
  264.8 2.4 constant_dynamic-update-slice_fusion.10
  276.9 2.3 bitcast_dynamic-update-slice_fusion.6
  282.9 6.0 %slice_dynamic-update-slice_fusion = (bf16[8,5,256,256]{2,3,0,1:T(8,128)(2,1)}, bf16[8,7,256,256]{2,3,0,1:T(8,128)(2,1)}, bf16[8,1,256,256]{2,3,0,1:T(8,128)(2,1...) fusion(bf16[8,5,256,256]{2,3,0,1:T(8,128)(2,1)} %get-tuple-elem, ...), kind=kLoop, calls=%fused_computation.49 | loop fusion | bytes 14680064 | tf_op jit(solution)/shard_map/stack | solution.py:58
  291.7 2.3 copy.140
  294.0 2.3 copy.137
  296.2 2.4 constant_dynamic-update-slice_fusion.16
  298.6 2.3 bitcast_dynamic-update-slice_fusion.5
  300.9 2.3 constant_dynamic-update-slice_fusion.23
  305.3 3.1 bitcast_dynamic-update-slice_fusion
  310.7 2.3 slice_dynamic-update-slice_fusion.1
  315.5 5.9 %constant_dynamic-update-slice_fusion.12 = (bf16[8,8,256,256]{3,2,0,1:T(8,128)(2,1)}, bf16[8,9,256,256]{3,2,0,1:T(8,128)(2,1)}) fusion(bf16[8,8,256,256]{3,2,0,1:T(8,128)(2,1)} %get-tuple-element.43, bf16[8,9,256,256]{3,2,0,1:T(8,128)(2,1)} %get-tuple-element.45, pred[8,4]{0,1:T(4,128)(4,1)S(1)} %fusion.47, bf16[8,5,256,256]{3,2,1,0:T(8,128)(2,1)} %bitcast.187), kind=kLoop, calls=%fused_computation.84 | loop fusion | flops 2097152 | bytes 12582944 | tf_op jit(solution)/shard_map/stack | solution.py:57
  321.4 9.0 %fusion.29 = bf16[8,5,256,256]{3,2,0,1:T(8,128)(2,1)S(1)} fusion(bf16[8,9,256,256]{3,2,0,1:T(8,128)(2,1)} %get-tuple-element.42, bf16[8,9,256,256]{3,2,0,1:T(8,128)(2,1)} %bitcast_dynamic-update-slice_fusion.6), kind=kOutput, calls=%fused_computation.39 | convolution fusion | flops 2416443392 | bytes 19922944 | tf_op jit(solution)/shard_map/rkab,rkbc->rac/dot_general | solution.py:59
  331.4 8.2 %fusion.31 = bf16[8,5,256,256]{3,2,0,1:T(8,128)(2,1)S(1)} fusion(bf16[8,5,256,256]{3,2,0,1:T(8,128)(2,1)S(1)} %fusion.29, bf16[8,8,256,256]{3,2,0,1:T(8,128)(2,1)} %get-tuple-element.41, bf16[8,8,256,256]{3,2,0,1:T(8,128)(2,1)} %bitcast_dynamic-update-slice_fusion.3, pred[8]{0:T(512)(128)(4,1)S(1)} %get-tuple-element.49), kind=kOutput, calls=%fused_computation.41 | convolution fusion | flops 2148532224 | bytes 17826304 | tf_op jit(solution)/shard_map/rkab,rkbc->rac/dot_general | solution.py:59
  339.7 4.4 fusion.35
  344.1 2.3 copy-done.6
  346.5 5.7 %fusion.41 = bf16[8,5,256,256]{3,2,0,1:T(8,128)(2,1)} fusion(bf16[8,5,256,256]{3,2,0,1:T(8,128)(2,1)} %copy-done.6, bf16[8,6,256,256]{3,2,0,1:T(8,128)(2,1)} %get-tuple-element.12, bf16[8,4,256,256]{3,2,0,1:T(8,128)(2,1)S(1)} %copy-done.5, bf16[8,1,256,256]{3,2,0,1:T(8,128)(2,1)S(1)} %fusion.46, bf16[8,1,256,256]{3,2,0,1:T(8,128)(2,1)S(1)} %copy-done.11, ...), kind=kOutput, calls=%fused_computation.45 | convolution fusion | flops 1617952768 | bytes 13631496 | tf_op jit(solution)/shard_map/rkab,rkbc->rac/dot_general | solution.py:59
  352.2 5.4 %fusion.45 = bf16[8,5,256,256]{3,2,0,1:T(8,128)(2,1)} fusion(bf16[8,5,256,256]{3,2,0,1:T(8,128)(2,1)} %fusion.41, bf16[8,5,256,256]{2,3,0,1:T(8,128)(2,1)} %get-tuple-element.5, bf16[8,1,256,256]{2,3,0,1:T(8,128)(2,1)S(1)} %copy.106, bf16[8,4,256,256]{2,3,0,1:T(8,128)(2,1)S(1)} %copy-done.3, pred[8]{0:T(512)(128)(4,1)S(1)} %get-tuple-element.46), kind=kOutput, calls=%fused_computation.47 | convolution fusion | flops 1345847296 | bytes 11534344 | tf_op jit(solution)/shard_map/rkab,rkbc->rac/dot_general | solution.py:59
  357.6 5.5 %copy.130 = bf16[8,5,256,256]{3,0,1,2:T(8,128)(2,1)S(1)} copy(bf16[8,5,256,256]{3,2,0,1:T(8,128)(2,1)} %fusion.45) | data formatting | bytes 10485760 | tf_op jit(solution)/shard_map/stack | solution.py:67
  363.1 120.7 %all_to_all.36 = bf16[8,5,256,256]{3,0,1,2:T(8,128)(2,1)S(1)} all-to-all(bf16[8,5,256,256]{3,0,1,2:T(8,128)(2,1)S(1)} %copy.130), channel_id=1, replica_groups=mesh['row'=4,'col'=8] {'col'}, dimensions={2} | all-to-all | bytes 10485760 | tf_op jit(solution)/shard_map/all_to_all | solution.py:81
  483.8 3.7 copy.131
  (62 shorter events, 47.5 us)
Async XLA Ops:
  0.0 5.8 %copy-start.13 = (s32[8,4]{0,1:T(4,128)S(1)}, s32[8,4]{0,1:T(4,128)}, u32[]{:S(2)}) copy-start(s32[8,4]{0,1:T(4,128)} %param.3) | copy-start | bytes 388
  0.0 118.7 %all-to-all-start = ((bf16[64,5,32,256]{3,2,1,0:T(8,128)(2,1)}), bf16[64,5,32,256]{3,2,1,0:T(8,128)(2,1)}, u32[]{:S(2)}, u32[]{:S(2)}) async-start(bf16[64,5,32,256]{3,2,1,0:T(8,128)(2,1)} %param.2), calls=%async_computation | async-start | bytes 10485760 | tf_op jit(solution)/shard_map/all_to_all | solution.py:71
  122.0 2.3 copy-start.4
  138.4 8.4 %copy-start.2 = (bf16[8,4,256,256]{2,3,0,1:T(8,128)(2,1)S(1)}, bf16[8,4,256,256]{2,3,0,1:T(8,128)(2,1)}, u32[]{:S(2)}) copy-start(bf16[8,4,256,256]{2,3,0,1:T(8,128)(2,1)} %copy.107) | copy-start | bytes 12582916
  141.0 53.0 %collective-permute-start.1 = (bf16[4,5,256,256]{2,3,0,1:T(8,128)(2,1)S(1)}, bf16[4,5,256,256]{2,3,0,1:T(8,128)(2,1)S(1)}, u32[]{:S(2)}, u32[]{:S(2)}) collective-permute-start(bf16[4,5,256,256]{2,3,0,1:T(8,128)(2,1)S(1)} %get-tuple-element.33), channel_id=1, source_target_pairs={{1,0},{2,1},{3,2},{4,3},{5,4},{6,5},{7,6},{8,7},{9,8},{10,9},{11,1... | collective-permute-start | bytes 7864328 | tf_op jit(solution)/shard_map/ppermute | solution.py:17
  143.3 59.9 %collective-permute-start = (bf16[4,5,256,256]{2,3,0,1:T(8,128)(2,1)S(1)}, bf16[4,5,256,256]{2,3,0,1:T(8,128)(2,1)S(1)}, u32[]{:S(2)}, u32[]{:S(2)}) collective-permute-start(bf16[4,5,256,256]{2,3,0,1:T(8,128)(2,1)S(1)} %get-tuple-element.34), channel_id=1, source_target_pairs={{0,1},{1,2},{2,3},{3,4},{4,5},{5,6},{6,7},{7,8},{8,9},{9,10},{10,1... | collective-permute-start | bytes 7864328 | tf_op jit(solution)/shard_map/ppermute | solution.py:15
  204.9 11.5 %copy-start = (bf16[12,5,256,256]{2,3,0,1:T(8,128)(2,1)}, bf16[12,5,256,256]{2,3,0,1:T(8,128)(2,1)S(1)}, u32[]{:S(2)}) copy-start(bf16[12,5,256,256]{2,3,0,1:T(8,128)(2,1)S(1)} %get-tuple-element.32) | copy-start | bytes 23592964
  204.9 11.4 %copy-start.1 = (bf16[12,5,256,256]{2,3,0,1:T(8,128)(2,1)}, bf16[12,5,256,256]{2,3,0,1:T(8,128)(2,1)S(1)}, u32[]{:S(2)}) copy-start(bf16[12,5,256,256]{2,3,0,1:T(8,128)(2,1)S(1)} %get-tuple-element.31) | copy-start | bytes 23592964
  264.8 8.9 %copy-start.9 = (bf16[8,1,256,256]{3,2,0,1:T(8,128)(2,1)S(1)}, bf16[8,1,256,256]{3,2,0,1:T(8,128)(2,1)}, u32[]{:S(2)}) copy-start(bf16[8,1,256,256]{3,2,0,1:T(8,128)(2,1)} %copy.113) | copy-start | bytes 3145732
  264.8 10.0 %copy-start.8 = (bf16[8,1,256,256]{3,2,0,1:T(8,128)(2,1)S(1)}, bf16[8,1,256,256]{3,2,0,1:T(8,128)(2,1)}, u32[]{:S(2)}) copy-start(bf16[8,1,256,256]{3,2,0,1:T(8,128)(2,1)} %copy.114) | copy-start | bytes 3145732
  264.8 11.0 %copy-start.7 = (bf16[8,1,256,256]{3,2,0,1:T(8,128)(2,1)S(1)}, bf16[8,1,256,256]{3,2,0,1:T(8,128)(2,1)}, u32[]{:S(2)}) copy-start(bf16[8,1,256,256]{3,2,0,1:T(8,128)(2,1)} %copy.115) | copy-start | bytes 3145732
  296.2 8.0 %copy-start.10 = (bf16[8,1,256,256]{3,2,0,1:T(8,128)(2,1)S(1)}, bf16[8,1,256,256]{3,2,0,1:T(8,128)(2,1)}, u32[]{:S(2)}) copy-start(bf16[8,1,256,256]{3,2,0,1:T(8,128)(2,1)} %copy.140) | copy-start | bytes 3145732
  331.4 8.3 %copy-start.5 = (bf16[8,4,256,256]{3,2,0,1:T(8,128)(2,1)S(1)}, bf16[8,4,256,256]{3,2,0,1:T(8,128)(2,1)}, u32[]{:S(2)}) copy-start(bf16[8,4,256,256]{3,2,0,1:T(8,128)(2,1)} %copy_select_fusion) | copy-start | bytes 12582916
  331.4 8.3 %copy-start.11 = (bf16[8,1,256,256]{3,2,0,1:T(8,128)(2,1)S(1)}, bf16[8,1,256,256]{3,2,0,1:T(8,128)(2,1)}, u32[]{:S(2)}) copy-start(bf16[8,1,256,256]{3,2,0,1:T(8,128)(2,1)} %get-tuple-element.16) | copy-start | bytes 3145732
  331.4 8.3 %copy-start.12 = (bf16[8,1,256,256]{3,2,0,1:T(8,128)(2,1)S(1)}, bf16[8,1,256,256]{3,2,0,1:T(8,128)(2,1)}, u32[]{:S(2)}) copy-start(bf16[8,1,256,256]{3,2,0,1:T(8,128)(2,1)} %get-tuple-element.15) | copy-start | bytes 3145732
  344.1 2.3 copy-start.6
  346.5 5.7 %copy-start.3 = (bf16[8,4,256,256]{2,3,0,1:T(8,128)(2,1)S(1)}, bf16[8,4,256,256]{2,3,0,1:T(8,128)(2,1)}, u32[]{:S(2)}) copy-start(bf16[8,4,256,256]{2,3,0,1:T(8,128)(2,1)} %copy.107) | copy-start | bytes 12582916
where the time goes:
time: 491 us; the launch traced here: 488 us
  waiting for transfers between devices  168 us (34%)
  local copies, waits for them, and re-layouts  139 us (28%)
  blocking collectives  121 us (25%)
  matrix products  32.8 us (7%)
  other arithmetic  15.2 us (3%)
  starting transfers between devices  11.5 us (2%)
    all_to_all x1, blocking collectives, shards(): lax.all_to_all(product, 'col', split_axis=2, concat_axis=0, tiled=True)  121 us
    all_to_all x1, waiting for transfers between devices, shards(): lax.all_to_all(upper_tiles, 'col', split_axis=0, concat_axis=2, tiled=True)  113 us
    unnamed x62, local copies, waits for them, and re-layouts  72.3 us
    ppermute x1, waiting for transfers between devices, extended_2(): lax.ppermute(head, axis, [((i + 1) % count, i) for i in range(ends)])  46.1 us
    dot_general x5, matrix products, square_band(): jnp.einsum('rkab,rkbc->rac', left_stack, right_stack, preferred_element_t...  32.8 us
    another operation x8, local copies, waits for them, and re-layouts, square_band(): right_stack = jnp.stack(rights, axis=1)  21.5 us
    slice x5, local copies, waits for them, and re-layouts, square_band(): right = extended[start:start + block_rows, rest]  12.1 us
  transfers between devices with their start and end apart: 3, of which 3 were waited for; matrix products, arithmetic and copies ran while one was open for 0% of the time, Pallas kernels for 0%

commit v1 on v0

v1 whole, which is shorter than its diff:
```python
import functools

import jax
import jax.numpy as jnp
from jax import lax
from jax.experimental import pallas as pl
from jax.experimental.pallas import tpu as pltpu
from jax.sharding import PartitionSpec as P

MESH = pl.DeviceIdType.MESH


def band_square_kernel(
    rows_n,
    cols_n,
    width,
    up,
    occ,
    out,
    tiles,
    strip,
    prod,
    occ_v,
    kept,
    in_send,
    in_recv,
    halo_send,
    halo_recv,
    out_send,
    out_recv,
    occ_sem,
    loc_sem,
):
    block_rows, block = tiles.shape[0], tiles.shape[2]
    slab = block // cols_n
    row, col = lax.axis_index("row"), lax.axis_index("col")
    odd = lax.rem(row, 2)

    def turned(c):
        return jnp.where(odd == 1, cols_n - 1 - c, c)

    pos = turned(col)
    chunk = row * cols_n + pos
    step = 1 - 2 * odd
    has_next, has_prev = chunk < rows_n * cols_n - 1, chunk > 0
    next_out, prev_out = pos == cols_n - 1, pos == 0
    next_dev = (jnp.where(next_out, row + 1, row), jnp.where(next_out, col, col + step))
    prev_dev = (jnp.where(prev_out, row - 1, row), jnp.where(prev_out, col, col - step))

    def other(k):
        return lax.rem(col + k, cols_n)

    barrier = pltpu.get_barrier_semaphore()

    @pl.loop(1, cols_n)
    def _(k):
        pl.semaphore_signal(barrier, inc=1, device_id=(row, other(k)), device_id_type=MESH)

    @pl.when(next_out & has_next)
    def _():
        pl.semaphore_signal(barrier, inc=1, device_id=next_dev, device_id_type=MESH)

    @pl.when(prev_out & has_prev)
    def _():
        pl.semaphore_signal(barrier, inc=1, device_id=prev_dev, device_id_type=MESH)

    outside = (next_out & has_next) | (prev_out & has_prev)
    pl.semaphore_wait(barrier, cols_n - 1 + jnp.where(outside, 1, 0))

    def slab_of(c):
        return pl.ds(pl.multiple_of(c * slab, slab), slab)

    def spans(part):
        for r in range(block_rows):
            cut = width - r if r < width else block_rows - r
            first = r < width
            yield r, (0 if first == (part == 0) else cut), (cut if first == (part == 0) else width + 1)

    mine = slab_of(col)
    for part in range(2):
        for r, lo, hi in spans(part):
            pltpu.make_async_copy(
                up.at[pos * block_rows + r, lo:hi], tiles.at[r, lo:hi, mine, :], loc_sem.at[part]
            ).start()

            @pl.loop(1, cols_n)
            def _(k):
                dst = other(k)
                pltpu.make_async_remote_copy(
                    src_ref=up.at[turned(dst) * block_rows + r, lo:hi],
                    dst_ref=tiles.at[r, lo:hi, mine, :],
                    send_sem=in_send.at[dst],
                    recv_sem=in_recv.at[part, col],
                    device_id=(row, dst),
                    device_id_type=MESH,
                ).start()

    partner = cols_n - 1 - col
    occ_copy = pltpu.make_async_remote_copy(
        src_ref=occ,
        dst_ref=occ_v,
        send_sem=occ_sem.at[0],
        recv_sem=occ_sem.at[1],
        device_id=(row, partner),
        device_id_type=MESH,
    )

    @pl.when(odd == 1)
    def _():
        occ_copy.start()
        occ_copy.wait()

    @pl.when(odd == 0)
    def _():
        here = pltpu.make_async_copy(occ, occ_v, occ_sem.at[1])
        here.start()
        here.wait()

    shape = occ_v.shape
    index = (
        chunk * block_rows
        + lax.broadcasted_iota(jnp.int32, shape, 0)
        + lax.broadcasted_iota(jnp.int32, shape, 1)
        + 1
    )
    total = rows_n * cols_n * block_rows
    kept[...] = jnp.where((occ_v[...] == 1) & (index < total), 1, 0)

    def part_of(n):
        return slice(n * block, (n + 1) * block)

    @pl.when(jnp.logical_not(has_prev))
    def _():
        for q in range(width):
            strip[q, :, : (width - q) * block] = jnp.zeros(
                (block, (width - q) * block), strip.dtype
            )

    @pl.when(jnp.logical_not(has_next))
    def _():
        for m in range(width):
            strip[block_rows + m, :, width * block : (2 * width - m) * block] = jnp.zeros(
                (block, (width - m) * block), strip.dtype
            )

    def place(part):
        half = pl.ds(0, width)
        piece = tiles.at[half, :, mine, :]
        pltpu.make_async_copy(piece, piece, loc_sem.at[part]).wait()

        @pl.loop(1, cols_n)
        def _(k):
            src = other(k)
            piece = tiles.at[half, :, slab_of(src), :]
            pltpu.make_async_copy(piece, piece, in_recv.at[part, src]).wait()

        for d in range(width + 1):

            @pl.loop(part * width, (part + 1) * width)
            def _(j):
                r = lax.rem(j + block_rows - d, block_rows)
                tile = tiles[r, d]
                if d == 0:
                    full = tile.astype(jnp.float32)
                    strip[r, :, part_of(width)] = (0.5 * (full + full.T)).astype(strip.dtype)
                else:
                    flag = kept[pl.ds(r, 1), :][:, d - 1 : d]
                    tile = jnp.where(flag == 1, tile, jnp.zeros_like(tile))
                    strip[r, :, part_of(width + d)] = tile
                    strip[r + d, :, part_of(width - d)] = tile.T

    def halo(way, m):
        if way == 0:
            cut = slice(0, (width - m) * block)
            src, dst, dev = block_rows + m, m, next_dev
        else:
            cut = slice(width * block, (2 * width - m) * block)
            src, dst, dev = m, block_rows + m, prev_dev
        return pltpu.make_async_remote_copy(
            src_ref=strip.at[src, :, cut],
            dst_ref=strip.at[dst, :, cut],
            send_sem=halo_send.at[way, m],
            recv_sem=halo_recv.at[way, m],
            device_id=dev,
            device_id_type=MESH,
        )

    place(0)

    @pl.when(has_next)
    def _():
        for m in range(width):
            halo(0, m).start()

    @pl.when(has_prev)
    def _():
        for m in range(width):
            halo(1, m).start()

    place(1)

    @pl.when(has_prev)
    def _():
        for m in range(width):
            halo(0, m).wait_recv()

    @pl.when(has_next)
    def _():
        for m in range(width):
            halo(1, m).wait_recv()

    for d in range(1, width):

        @pl.loop(block_rows, block_rows + width - d)
        def _(r):
            strip[r + d, :, part_of(width - d)] = strip[r, :, part_of(width + d)].T

    @pl.loop(0, block_rows)
    def _(r):
        flags = kept[pl.ds(r, 1), :]
        for e in range(width + 1):
            value = lax.dot_general(
                strip[r, :, e * block :],
                strip[r + e, :, : (2 * width + 1 - e) * block],
                (((1,), (1,)), ((), ())),
                preferred_element_type=jnp.float32,
            )
            if e > 0:
                value = jnp.where(flags[:, e - 1 : e] == 1, value, 0.0)
            prod[r, e] = value.astype(prod.dtype)
        place_row = pos * block_rows + r
        pltpu.make_async_copy(prod.at[r, :, mine, :], out.at[place_row], loc_sem.at[2]).start()

        @pl.loop(1, cols_n)
        def _(k):
            dst = other(k)
            pltpu.make_async_remote_copy(
                src_ref=prod.at[r, :, slab_of(dst), :],
                dst_ref=out.at[place_row],
                send_sem=out_send.at[dst],
                recv_sem=out_recv.at[col],
                device_id=(row, dst),
                device_id_type=MESH,
            ).start()

    @pl.when(has_next)
    def _():
        for m in range(width):
            halo(0, m).wait_send()

    @pl.when(has_prev)
    def _():
        for m in range(width):
            halo(1, m).wait_send()

    def rows_of(c):
        return pl.ds(turned(c) * block_rows, block_rows)

    whole = out.at[rows_of(col)]
    pltpu.make_async_copy(whole, whole, loc_sem.at[2]).wait()

    @pl.loop(1, cols_n)
    def _(k):
        dev = other(k)
        sent = up.at[rows_of(dev)]
        pltpu.make_async_copy(sent, sent, in_send.at[dev]).wait()
        left = prod.at[:, :, slab_of(dev), :]
        pltpu.make_async_copy(left, left, out_send.at[dev]).wait()
        came = out.at[rows_of(dev)]
        pltpu.make_async_copy(came, came, out_recv.at[dev]).wait()


def shards(rows_n, cols_n, upper_tiles, occupied):
    block_rows, width = occupied.shape
    block = upper_tiles.shape[3]
    flags = jnp.pad(occupied, ((0, 0), (0, 128 - width)))
    dma = pltpu.SemaphoreType.DMA
    return pl.pallas_call(
        functools.partial(band_square_kernel, rows_n, cols_n, width),
        out_shape=jax.ShapeDtypeStruct(upper_tiles.shape, upper_tiles.dtype),
        in_specs=[pl.BlockSpec(memory_space=pl.ANY)] * 2,
        out_specs=pl.BlockSpec(memory_space=pl.ANY),
        scratch_shapes=[
            pltpu.VMEM((block_rows, width + 1, block, block), jnp.bfloat16),
            pltpu.VMEM((block_rows + width, block, (2 * width + 1) * block), jnp.bfloat16),
            pltpu.VMEM((block_rows, width + 1, block, block), jnp.bfloat16),
            pltpu.VMEM((block_rows, 128), jnp.int32),
            pltpu.VMEM((block_rows, 128), jnp.int32),
            dma((cols_n,)),
            dma((2, cols_n)),
            dma((2, width)),
            dma((2, width)),
            dma((cols_n,)),
            dma((cols_n,)),
            dma((2,)),
            dma((3,)),
        ],
        compiler_params=pltpu.CompilerParams(
            collective_id=0, has_side_effects=True, vmem_limit_bytes=48 * 2**20
        ),
        cost_estimate=pl.CostEstimate(
            flops=2 * 35 * block_rows * block**3, bytes_accessed=2 * upper_tiles.size * 2, transcendentals=0
        ),
    )(upper_tiles, flags)


def solution(mesh):
    return jax.shard_map(
        functools.partial(shards, mesh.shape["row"], mesh.shape["col"]),
        mesh=mesh,
        in_specs=(P("row", None, "col", None), P(("row", "col"), None)),
        out_specs=P("row", None, "col", None),
        check_vma=False,
    )
```

time: 491 us -> 253 us (0.52)
  Pallas kernels: 0 us -> 250 us
  waiting for transfers between devices: 168 us -> 0 us
  local copies, waits for them, and re-layouts: 139 us -> 3.12 us
  blocking collectives: 121 us -> 0 us
  matrix products: 32.8 us -> 0 us
  other arithmetic: 15.2 us -> 0 us
  starting transfers between devices: 11.5 us -> 0 us
    pallas_call x0 -> x1, Pallas kernels: none -> 250 us  [shards(): pl.pallas_call(functools.partial(band_square_kernel, rows_n, cols_n, widt...]
    all_to_all x1 -> x0, blocking collectives: 121 us -> none  [shards(): lax.all_to_all(product, 'col', split_axis=2, concat_axis=0, tiled=True)]
    all_to_all x1 -> x0, waiting for transfers between devices: 113 us -> none  [shards(): lax.all_to_all(upper_tiles, 'col', split_axis=0, concat_axis=2, tiled=True)]
    unnamed x62 -> x2, local copies, waits for them, and re-layouts: 72.3 us -> 3.12 us
    ppermute x2 -> x0, waiting for transfers between devices: 55.4 us -> none  [the longest x1 46.1 us: extended_2(): lax.ppermute(head, axis, [((i + 1) % count, i) for i in range(ends)])]
    dot_general x5 -> x0, matrix products: 32.8 us -> none  [square_band(): jnp.einsum('rkab,rkbc->rac', left_stack, right_stack, preferred_element_t...]
    another operation x9 -> x0, local copies, waits for them, and re-layouts: 27 us -> none  [the longest x8 21.5 us: square_band(): right_stack = jnp.stack(rights, axis=1)]
    slice x12 -> x0, local copies, waits for them, and re-layouts: 24 us -> none  [the longest x5 12.1 us: square_band(): right = extended[start:start + block_rows, rest]]
  transfers between devices with their start and end apart: 3 -> 0, of which waited for: 3 -> 0; matrix products, arithmetic and copies ran while one was open for 0% -> 0% of each run, Pallas kernels for 0% -> 0%
where the time goes in v1:
time: 253 us
  Pallas kernels  250 us (99%)
  local copies, waits for them, and re-layouts  3.12 us (1%)
    pallas_call x1, Pallas kernels, shards(): pl.pallas_call(functools.partial(band_square_kernel, rows_n, cols_n, widt...  250 us

profile of v1, /device:TPU:11, one launch (start us, length us, event | category | flops | bytes accessed | tf_op | source)
XLA Modules:
  0.0 253.1 jit_solution(14011531326773016495)
XLA Ops:
  0.0 0.8 copy.3
  0.8 250.0 %shard_map.28 = bf16[64,5,32,256]{3,2,1,0:T(8,128)(2,1)S(1)} custom-call(bf16[64,5,32,256]{3,2,1,0:T(8,128)(2,1)} %up.1, s32[8,128]{1,0:T(8,128)S(1)} %pad.4.occ), custom_call_target="tpu_custom_call" | custom-call | flops 9395240960 | bytes 10485760 | tf_op jit(solution)/shard_map/pallas_call | solution.py:278
  250.7 2.4 copy.5
  (1 shorter events, 0.0 us)
